TPU v7x, 32 devices: a whole 2x2x4 slice. The times are simulated.
32 devices in a mesh: grp: 2 (over x), tm: 16 (over z, y, core).
Axes of the slice: x: 2, y: 2, z: 4, core: 2. Of those that a mesh axis runs over, the one named last changes fastest.
Arguments:
- noise: float32 [32, 256, 256], P(('grp', 'tm')), parts along dimension 0, may hold values from -6 to 6
- phonon_level: int32 [32, 256, 256], P(('grp', 'tm')), parts along dimension 0, may hold values from 0 to 16
- hop_x: float32 [256, 256], replicated, as said below
- hop_y: float32 [256, 256], replicated, as said below
Outputs:
- solution: float32 [32, 256, 256], P(('grp', 'tm')), parts along dimension 0
- residual: float32 [32, 256, 256], P(('grp', 'tm')), parts along dimension 0
There are 2 independent parts, one for each index of `grp`. A program takes and returns all parts, laid end to end along the dimension named above; an argument that names none is the same for every part. Nothing has to cross between parts.
Inputs may be any that keep to these rules, and one draw needn't show every extreme that they name: hop_x is symmetric. hop_y is symmetric.
All inputs are finite; a program needn't handle non-finite values.
Results may differ from a plain program's by a relative error of at most 0.0003.
Values sent between devices are 32-bit elements; how exact they have to be, the bound alone decides.
A program may use at most 64 MiB of HBM per device.

v0:
```python
import functools
import math

import jax
import jax.numpy as jnp
from jax import lax
from jax.experimental import pallas as pl
from jax.experimental.pallas import tpu as pltpu
from jax.sharding import PartitionSpec as P

ORDER = 10
LEVELS = 17


def from_behind(value, axis, steps):
    count = lax.axis_size(axis)
    pairs = [(source, (source + steps) % count) for source in range(count)]
    return lax.ppermute(value, axis, pairs)


def propagate(field, hop_x, hop_y):
    inner = jnp.einsum("ax,nxy->nay", hop_x, field, precision=lax.Precision.HIGHEST)
    return jnp.einsum("nay,yb->nab", inner, hop_y, precision=lax.Precision.HIGHEST)


def normal_apply(vector, damp, hop_x, hop_y):
    num_devices = lax.axis_size("tm")
    position = lax.axis_index("tm")
    incoming = from_behind(vector, "tm", 1)
    incoming = incoming * jnp.where(position == 0, -1.0, 1.0).astype(jnp.float32)
    previous = jnp.concatenate([incoming, vector[:-1]], axis=0)
    forward = vector - propagate(damp * previous, hop_x, hop_y)
    carried = damp * propagate(forward, hop_x, hop_y)
    returning = from_behind(carried, "tm", -1)
    returning = returning * jnp.where(position == num_devices - 1, -1.0, 1.0).astype(jnp.float32)
    following = jnp.concatenate([carried[1:], returning], axis=0)
    return forward - following


def chebyshev(field, cosines, cbar, hop_x, hop_y):
    lower_edge = 0.05
    upper_edge = (1.0 + 3.0 * cbar) ** 2
    center = (upper_edge + lower_edge) / (upper_edge - lower_edge)
    radius_term = jnp.sqrt(center * center - 1.0)
    ratio = center - radius_term
    cos_block = cosines[:, None, None]

    def apply_shifted(vector):
        once = propagate(vector, hop_x, hop_y)
        twice = propagate(once, hop_x, hop_y)
        normal_part = vector + cbar * cbar * twice - 2.0 * cbar * cos_block * once
        return (2.0 * normal_part - (upper_edge + lower_edge) * vector) / (upper_edge - lower_edge)

    previous = field
    current = apply_shifted(field)
    weight = -ratio
    total_sum = previous + 2.0 * weight * current
    for degree in range(2, ORDER + 1):
        following = 2.0 * apply_shifted(current) - previous
        weight = weight * -ratio
        total_sum = total_sum + 2.0 * weight * following
        previous = current
        current = following
    return total_sum * (2.0 / ((upper_edge - lower_edge) * radius_term))


def precondition(resid, cbar, hop_x, hop_y):
    slices = resid.shape[0]
    side_x = resid.shape[1]
    side_y = resid.shape[2]
    num_devices = lax.axis_size("tm")
    length = slices * num_devices
    position = lax.axis_index("tm")
    flat = resid.reshape(slices, side_x * side_y)
    slab = lax.all_to_all(flat, "tm", split_axis=1, concat_axis=0, tiled=True)
    times = jnp.arange(length, dtype=jnp.int32)
    local_rows = position * slices + jnp.arange(slices, dtype=jnp.int32)
    freq_rows = times // 2
    phase = (2 * freq_rows[:, None] + 1) * times[None, :] % (2 * length)
    angles = phase.astype(jnp.float32) * (math.pi / length)
    basis_table = jnp.where((times % 2 == 0)[:, None], jnp.cos(angles), jnp.sin(angles))
    spectrum = jnp.dot(basis_table, slab, precision=lax.Precision.HIGHEST)
    components = lax.all_to_all(spectrum, "tm", split_axis=0, concat_axis=1, tiled=True)
    cosines = jnp.cos((2 * (local_rows // 2) + 1).astype(jnp.float32) * (math.pi / length))
    result = chebyshev(components.reshape(slices, side_x, side_y), cosines, cbar, hop_x, hop_y)
    returned = lax.all_to_all(
        result.reshape(slices, side_x * side_y), "tm", split_axis=1, concat_axis=0, tiled=True
    )
    back = jnp.dot(basis_table.T, returned, precision=lax.Precision.HIGHEST) * (2.0 / length)
    timeline = lax.all_to_all(back, "tm", split_axis=0, concat_axis=1, tiled=True)
    return timeline.reshape(slices, side_x, side_y)


def halves(value):
    high = value.astype(jnp.bfloat16)
    low = (value - high.astype(jnp.float32)).astype(jnp.bfloat16)
    return high, low


def left_stack(matrix):
    high, low = halves(matrix)
    return jnp.concatenate([high, high, low], axis=1)


def right_stack(matrix):
    high, low = halves(matrix)
    return jnp.concatenate([high, low, high], axis=0)


def product(left, right):
    return jnp.dot(left, right, preferred_element_type=jnp.float32)


def exact(left, right):
    return jnp.dot(left, right, precision=lax.Precision.HIGHEST, preferred_element_type=jnp.float32)


def fused_kernel(
    n, noise_ref, level_ref, hx_ref, hy_ref, tab_ref, cos_ref, sol_ref, res_ref,
    slab, spec, comp, zbuf, back, line, step, second, prev, carr, foll, vec, part, parts,
    left_ref, right_ref, hop_left, hop_right,
    a2a_send, a2a_recv, hop_send, hop_recv, sum_send, sum_recv,
):
    me = lax.axis_index("tm")
    side_x, side_y = hx_ref.shape[0], hy_ref.shape[0]
    rows = noise_ref.shape[1]
    whole = (side_x, side_y)
    blocks = (n, rows, side_y)

    barrier = pltpu.get_barrier_semaphore()

    def greet(i, carry):
        pl.semaphore_signal(
            barrier, inc=1, device_id={"tm": lax.rem(me + i, n)}, device_id_type=pl.DeviceIdType.MESH
        )
        return carry

    lax.fori_loop(1, n, greet, 0)
    pl.semaphore_wait(barrier, n - 1)

    def push(src, dst, send, recv, target):
        pltpu.make_async_remote_copy(
            src_ref=src, dst_ref=dst, send_sem=send, recv_sem=recv,
            device_id={"tm": target}, device_id_type=pl.DeviceIdType.MESH,
        ).start()

    def bytes_of(ref, sem):
        pltpu.make_async_copy(ref, ref, sem).wait()

    def scatter(src, dst, which):
        def one(i, carry):
            j = lax.rem(me + i, n)
            push(src.at[j], dst.at[me], a2a_send.at[which], a2a_recv.at[which], j)
            return carry

        lax.fori_loop(1, n, one, 0)
        dst[me] = src[me]

    def arrived(dst, which):
        bytes_of(dst.at[pl.ds(0, n - 1)], a2a_recv.at[which])

    def sent(src, which):
        bytes_of(src.at[pl.ds(0, n - 1)], a2a_send.at[which])

    def mix(source, j, entry):
        total = entry(j, 0) * source[0]
        for t in range(1, n):
            total = total + entry(j, t) * source[t]
        return total

    def mix_scatter(source, staged, dst, which, entry):
        def one(i, carry):
            j = lax.rem(me + i, n)
            staged[j] = mix(source, j, entry)
            push(staged.at[j], dst.at[me], a2a_send.at[which], a2a_recv.at[which], j)
            return carry

        lax.fori_loop(1, n, one, 0)
        dst[me] = mix(source, me, entry)

    forward_entry = lambda j, t: tab_ref[j, t]
    backward_entry = lambda j, t: tab_ref[t, j]

    scatter(noise_ref, slab.at[0], 0)

    levels = level_ref[...].astype(jnp.float32)
    middle = (LEVELS - 1) // 2
    folded = jnp.sum(levels.reshape(side_x // 8, 8, side_y), axis=0)
    lanes = part.shape[1]
    partial = folded[:, :lanes]
    for start in range(lanes, side_y, lanes):
        partial = partial + folded[:, start : start + lanes]
    part[...] = partial

    def share(i, carry):
        j = lax.rem(me + i, n)
        push(part, parts.at[me], sum_send, sum_recv, j)
        return carry

    lax.fori_loop(1, n, share, 0)
    parts[me] = part[...]

    hop_x = hx_ref[...]
    hop_y = hy_ref[...]
    hop_left[...] = left_stack(hop_x)
    hop_right[...] = right_stack(hop_y)
    left_ref[0:side_x] = hop_left[...]
    left_ref[side_x : 2 * side_x] = left_stack(exact(hop_x, hop_x))
    hop_y_twice = exact(hop_y, hop_y)
    damp = jnp.exp(-0.05 * (levels - middle))

    def propagate_one(field):
        inner = product(hop_left[...], right_of(field))
        return product(left_of(inner), hop_right[...])

    def right_of(field):
        high, low = halves(field)
        return jnp.concatenate([high, low, high], axis=0)

    def left_of(field):
        high, low = halves(field)
        return jnp.concatenate([high, high, low], axis=1)

    def chebyshev_local(field, consts):
        linear, weight0, ratio, scale = consts

        def doubled(vector):
            inner = product(left_ref[...], right_of(vector))
            both = jnp.concatenate([left_of(inner[:side_x]), left_of(inner[side_x:])], axis=1)
            return linear * vector + product(both, right_ref[...])

        current = 0.5 * doubled(field)
        total = field + 2.0 * weight0 * current

        def body(degree, carry):
            previous, current, total, weight = carry
            following = doubled(current) - previous
            weight = weight * weight0
            return current, following, total + 2.0 * weight * following, weight

        _, _, total, _ = lax.fori_loop(2, ORDER + 1, body, (field, current, total, weight0))
        return total * scale

    consts = None
    sign_first = jnp.where(me == 0, -1.0, 1.0).astype(jnp.float32)
    sign_last = jnp.where(me == n - 1, -1.0, 1.0).astype(jnp.float32)
    after = lax.rem(me + 1, n)
    before = lax.rem(me + n - 1, n)
    noise = noise_ref[...].reshape(whole)
    held = None
    for turn in range(2):
        at = 4 * turn
        source = noise_ref if turn == 0 else second
        arrived(slab.at[turn], at)
        mix_scatter(slab.at[turn], spec.at[turn], comp.at[turn], at + 1, forward_entry)
        if turn == 0:
            bytes_of(parts.at[pl.ds(0, n - 1)], sum_recv)
            level_sum = jnp.sum(jnp.sum(parts[...], axis=0), axis=(0, 1), keepdims=True)
            mean_level = level_sum / (n * side_x * side_y)
            cbar = jnp.exp(-0.05 * (mean_level - middle))
            lower = 0.05
            upper = (1.0 + 3.0 * cbar) * (1.0 + 3.0 * cbar)
            width = upper - lower
            center = (upper + lower) / width
            radius = jnp.sqrt(center * center - 1.0)
            ratio = center - radius
            linear = 2.0 * (2.0 - (upper + lower)) / width
            once = -8.0 * cbar * cos_ref[me] / width
            twice = 4.0 * cbar * cbar / width
            scale = (2.0 / (width * radius)) * (2.0 / n)
            right_ref[0 : 3 * side_y] = right_stack(once * hop_y)
            right_ref[3 * side_y : 6 * side_y] = right_stack(twice * hop_y_twice)
            consts = (linear, -ratio, ratio, scale)
        arrived(comp.at[turn], at + 1)
        zbuf[turn] = chebyshev_local(comp[turn].reshape(whole), consts).reshape(blocks)
        scatter(zbuf.at[turn], back.at[turn], at + 2)
        arrived(back.at[turn], at + 2)
        mix_scatter(back.at[turn], line.at[turn], step.at[turn], at + 3, backward_entry)
        arrived(step.at[turn], at + 3)
        vector = step[turn].reshape(whole)
        if turn == 1:
            vector = vec[0] + vector
            sol_ref[...] = vector.reshape(blocks)
        vec[turn] = vector
        push(vec.at[turn], prev.at[turn], hop_send.at[2 * turn], hop_recv.at[2 * turn], after)
        bytes_of(prev.at[turn], hop_recv.at[2 * turn])
        forward = vector - propagate_one(damp * (sign_first * prev[turn]))
        carr[turn] = damp * propagate_one(forward)
        push(carr.at[turn], foll.at[turn], hop_send.at[2 * turn + 1], hop_recv.at[2 * turn + 1], before)
        bytes_of(foll.at[turn], hop_recv.at[2 * turn + 1])
        rest = noise - (forward - sign_last * foll[turn])
        if turn == 0:
            second[...] = rest.reshape(blocks)
            scatter(second, slab.at[1], 4)
        else:
            res_ref[...] = rest.reshape(blocks)

    for turn in range(2):
        at = 4 * turn
        sent(noise_ref if turn == 0 else second, at)
        sent(spec.at[turn], at + 1)
        sent(zbuf.at[turn], at + 2)
        sent(line.at[turn], at + 3)
        bytes_of(vec.at[turn], hop_send.at[2 * turn])
        bytes_of(carr.at[turn], hop_send.at[2 * turn + 1])
    bytes_of(parts.at[pl.ds(0, n - 1)], sum_send)


def fused(noise, phonon_level, hop_x, hop_y):
    n = lax.axis_size("tm")
    side_x, side_y = noise.shape[1], noise.shape[2]
    rows = side_x // n
    blocks = (n, rows, side_y)
    times = jnp.arange(n, dtype=jnp.int32)
    freqs = times // 2
    phase = (2 * freqs[:, None] + 1) * times[None, :] % (2 * n)
    angles = phase.astype(jnp.float32) * (math.pi / n)
    table = jnp.where((times % 2 == 0)[:, None], jnp.cos(angles), jnp.sin(angles))
    cosines = jnp.cos((2 * freqs + 1).astype(jnp.float32) * (math.pi / n))
    f32, bf16 = jnp.float32, jnp.bfloat16
    pair = pltpu.VMEM((2,) + blocks, f32)
    plane = pltpu.VMEM((2, side_x, side_y), f32)
    vmem = pl.BlockSpec(memory_space=pltpu.VMEM)
    smem = pl.BlockSpec(memory_space=pltpu.SMEM)
    dma = pltpu.SemaphoreType.DMA
    out = jax.ShapeDtypeStruct(blocks, f32)
    sol, res = pl.pallas_call(
        functools.partial(fused_kernel, n),
        out_shape=(out, out),
        in_specs=[vmem] * 4 + [smem] * 2,
        out_specs=(vmem, vmem),
        scratch_shapes=[pair] * 7
        + [pltpu.VMEM(blocks, f32)]
        + [plane] * 4
        + [pltpu.VMEM((8, 128), f32), pltpu.VMEM((n, 8, 128), f32)]
        + [
            pltpu.VMEM((2 * side_x, 3 * side_x), bf16),
            pltpu.VMEM((6 * side_y, side_y), bf16),
            pltpu.VMEM((side_x, 3 * side_x), bf16),
            pltpu.VMEM((3 * side_y, side_y), bf16),
        ]
        + [dma((8,)), dma((8,)), dma((4,)), dma((4,)), dma(()), dma(())],
        compiler_params=pltpu.CompilerParams(
            collective_id=0, has_side_effects=True, vmem_limit_bytes=40 * 1024 * 1024
        ),
    )(noise.reshape(blocks), phonon_level.reshape(side_x, side_y), hop_x, hop_y, table, cosines)
    return sol.reshape(noise.shape), res.reshape(noise.shape)


def per_device(noise, phonon_level, hop_x, hop_y):
    slices = noise.shape[0]
    num_devices = lax.axis_size("tm")
    if slices == 1 and noise.shape[1] % (8 * num_devices) == 0 and noise.shape[2] % 128 == 0:
        return fused(noise, phonon_level, hop_x, hop_y)
    middle = (LEVELS - 1) // 2
    levels = phonon_level.astype(jnp.float32)
    damp = jnp.exp(-0.05 * (levels - middle))
    level_sum = lax.psum(jnp.sum(levels), "tm")
    mean_level = level_sum / (slices * num_devices * noise.shape[1] * noise.shape[2])
    cbar = jnp.exp(-0.05 * (mean_level - middle))
    first = precondition(noise, cbar, hop_x, hop_y)
    second_residual = noise - normal_apply(first, damp, hop_x, hop_y)
    solution = first + precondition(second_residual, cbar, hop_x, hop_y)
    residual = noise - normal_apply(solution, damp, hop_x, hop_y)
    return (solution, residual)


def solution(mesh):
    return jax.shard_map(
        per_device,
        mesh=mesh,
        in_specs=(P(("grp", "tm"), None, None), P(("grp", "tm"), None, None), P(), P()),
        out_specs=(P(("grp", "tm"), None, None), P(("grp", "tm"), None, None)),
        check_vma=False,
    )
```

profile of v0, /device:TPU:0, one launch (start us, length us, event | category | flops | bytes accessed | tf_op | source)
XLA Modules:
  0.0 116.2 jit_solution(13049457464207708509)
XLA Ops:
  0.7 0.1 sine_select_fusion.tab_ref
  0.8 0.0 copy-start
  0.8 0.9 copy-done
  1.8 0.0 copy-start.1
  1.8 0.9 copy-done.1
  2.7 0.0 copy-start.2
  2.7 0.9 copy-done.2
  3.7 0.0 copy-start.3
  3.7 0.9 copy-done.3
  4.6 110.1 %shard_map.59 = (f32[16,16,256]{2,1,0:T(8,128)S(1)}, f32[16,16,256]{2,1,0:T(8,128)S(1)}) custom-call(f32[16,16,256]{2,1,0:T(8,128)S(1)} %bitcast.6, s32[256,256]{1,0:T(8,128)S(1)} %bitcast.7, f32[256,256]{1,0:T(8,128)S(1)} %copy-done.2, f32[256,256]{1,0:T(8,128)S(1)} %copy-done.3, f32[16,16]{1,0:T(8,128)S(1)} %sine_select_fusion.tab_ref, ...), custom_call_target="tpu_custom_call" | custom-call | tf_op jit(solution)/shard_map/pallas_call | solution.py:327
  114.8 0.7 copy.8
  115.5 0.7 copy.9
  (3 shorter events, 0.1 us)
Async XLA Ops:
  0.8 1.0 copy-start
  1.8 0.9 copy-start.1
  2.7 0.9 copy-start.2
  3.7 0.9 copy-start.3
where the time goes:
time: 116 us
  Pallas kernels  110 us (95%)
  local copies, waits for them, and re-layouts  5.2 us (4%)
    pallas_call x1, Pallas kernels, fused(): pl.pallas_call(functools.partial(fused_kernel, n), out_shape=(out, out),...  110 us
    unnamed x10, local copies, waits for them, and re-layouts  5.2 us

commit v1 on v0

--- a/solution.py
+++ b/solution.py
@@ -117,7 +117,8 @@
 
 def fused_kernel(
     n, noise_ref, level_ref, hx_ref, hy_ref, tab_ref, cos_ref, sol_ref, res_ref,
-    slab, spec, comp, zbuf, back, line, step, second, prev, carr, foll, vec, part, parts,
+    slab, spec, comp, zbuf, back, line, step, prev, carr, foll, vec,
+    second, work, held, damp_ref, part, parts,
     left_ref, right_ref, hop_left, hop_right,
     a2a_send, a2a_recv, hop_send, hop_recv, sum_send, sum_recv,
 ):
@@ -126,6 +127,9 @@
     rows = noise_ref.shape[1]
     whole = (side_x, side_y)
     blocks = (n, rows, side_y)
+    chunks = rows // 8
+    strip = (n, 8, side_y)
+    flat = (8 * n, side_y)
 
     barrier = pltpu.get_barrier_semaphore()
 
@@ -147,41 +151,51 @@
     def bytes_of(ref, sem):
         pltpu.make_async_copy(ref, ref, sem).wait()
 
-    def scatter(src, dst, which):
+    def span(h):
+        return pl.ds(8 * h, 8)
+
+    def scatter(src, dst, which, h):
         def one(i, carry):
             j = lax.rem(me + i, n)
-            push(src.at[j], dst.at[me], a2a_send.at[which], a2a_recv.at[which], j)
+            push(
+                src.at[j, span(h)], dst.at[me, span(h)],
+                a2a_send.at[which], a2a_recv.at[which, h], j,
+            )
             return carry
 
         lax.fori_loop(1, n, one, 0)
-        dst[me] = src[me]
-
-    def arrived(dst, which):
-        bytes_of(dst.at[pl.ds(0, n - 1)], a2a_recv.at[which])
+        dst[me, span(h)] = src[me, span(h)]
+
+    def arrived(dst, which, h):
+        bytes_of(dst.at[pl.ds(0, n - 1), span(h)], a2a_recv.at[which, h])
 
     def sent(src, which):
         bytes_of(src.at[pl.ds(0, n - 1)], a2a_send.at[which])
 
-    def mix(source, j, entry):
-        total = entry(j, 0) * source[0]
+    def mix(source, j, entry, h):
+        total = entry(j, 0) * source[0, span(h)]
         for t in range(1, n):
-            total = total + entry(j, t) * source[t]
+            total = total + entry(j, t) * source[t, span(h)]
         return total
 
-    def mix_scatter(source, staged, dst, which, entry):
+    def mix_scatter(source, staged, dst, which, entry, h):
         def one(i, carry):
             j = lax.rem(me + i, n)
-            staged[j] = mix(source, j, entry)
-            push(staged.at[j], dst.at[me], a2a_send.at[which], a2a_recv.at[which], j)
+            staged[j, span(h)] = mix(source, j, entry, h)
+            push(
+                staged.at[j, span(h)], dst.at[me, span(h)],
+                a2a_send.at[which], a2a_recv.at[which, h], j,
+            )
             return carry
 
         lax.fori_loop(1, n, one, 0)
-        dst[me] = mix(source, me, entry)
+        dst[me, span(h)] = mix(source, me, entry, h)
 
     forward_entry = lambda j, t: tab_ref[j, t]
     backward_entry = lambda j, t: tab_ref[t, j]
 
-    scatter(noise_ref, slab.at[0], 0)
+    for h in range(chunks):
+        scatter(noise_ref, slab.at[0], 0, h)
 
     levels = level_ref[...].astype(jnp.float32)
     middle = (LEVELS - 1) // 2
@@ -207,11 +221,7 @@
     left_ref[0:side_x] = hop_left[...]
     left_ref[side_x : 2 * side_x] = left_stack(exact(hop_x, hop_x))
     hop_y_twice = exact(hop_y, hop_y)
-    damp = jnp.exp(-0.05 * (levels - middle))
-
-    def propagate_one(field):
-        inner = product(hop_left[...], right_of(field))
-        return product(left_of(inner), hop_right[...])
+    damp_ref[...] = jnp.exp(-0.05 * (levels - middle)).reshape(blocks)
 
     def right_of(field):
         high, low = halves(field)
@@ -246,13 +256,11 @@
     sign_last = jnp.where(me == n - 1, -1.0, 1.0).astype(jnp.float32)
     after = lax.rem(me + 1, n)
     before = lax.rem(me + n - 1, n)
-    noise = noise_ref[...].reshape(whole)
-    held = None
     for turn in range(2):
         at = 4 * turn
-        source = noise_ref if turn == 0 else second
-        arrived(slab.at[turn], at)
-        mix_scatter(slab.at[turn], spec.at[turn], comp.at[turn], at + 1, forward_entry)
+        for h in range(chunks):
+            arrived(slab.at[turn], at, h)
+            mix_scatter(slab.at[turn], spec.at[turn], comp.at[turn], at + 1, forward_entry, h)
         if turn == 0:
             bytes_of(parts.at[pl.ds(0, n - 1)], sum_recv)
             level_sum = jnp.sum(jnp.sum(parts[...], axis=0), axis=(0, 1), keepdims=True)
@@ -271,29 +279,50 @@
             right_ref[0 : 3 * side_y] = right_stack(once * hop_y)
             right_ref[3 * side_y : 6 * side_y] = right_stack(twice * hop_y_twice)
             consts = (linear, -ratio, ratio, scale)
-        arrived(comp.at[turn], at + 1)
+        for h in range(chunks):
+            arrived(comp.at[turn], at + 1, h)
         zbuf[turn] = chebyshev_local(comp[turn].reshape(whole), consts).reshape(blocks)
-        scatter(zbuf.at[turn], back.at[turn], at + 2)
-        arrived(back.at[turn], at + 2)
-        mix_scatter(back.at[turn], line.at[turn], step.at[turn], at + 3, backward_entry)
-        arrived(step.at[turn], at + 3)
-        vector = step[turn].reshape(whole)
-        if turn == 1:
-            vector = vec[0] + vector
-            sol_ref[...] = vector.reshape(blocks)
-        vec[turn] = vector
-        push(vec.at[turn], prev.at[turn], hop_send.at[2 * turn], hop_recv.at[2 * turn], after)
-        bytes_of(prev.at[turn], hop_recv.at[2 * turn])
-        forward = vector - propagate_one(damp * (sign_first * prev[turn]))
-        carr[turn] = damp * propagate_one(forward)
-        push(carr.at[turn], foll.at[turn], hop_send.at[2 * turn + 1], hop_recv.at[2 * turn + 1], before)
-        bytes_of(foll.at[turn], hop_recv.at[2 * turn + 1])
-        rest = noise - (forward - sign_last * foll[turn])
-        if turn == 0:
-            second[...] = rest.reshape(blocks)
-            scatter(second, slab.at[1], 4)
-        else:
-            res_ref[...] = rest.reshape(blocks)
+        for h in range(chunks):
+            scatter(zbuf.at[turn], back.at[turn], at + 2, h)
+        for h in range(chunks):
+            arrived(back.at[turn], at + 2, h)
+            mix_scatter(back.at[turn], line.at[turn], step.at[turn], at + 3, backward_entry, h)
+        for h in range(chunks):
+            arrived(step.at[turn], at + 3, h)
+            fresh = step[turn, :, span(h)]
+            if turn == 1:
+                fresh = vec[0, :, span(h)] + fresh
+                sol_ref[:, span(h)] = fresh
+            vec[turn, :, span(h)] = fresh
+            push(
+                vec.at[turn, :, span(h)], prev.at[turn, :, span(h)],
+                hop_send.at[2 * turn], hop_recv.at[2 * turn, h], after,
+            )
+        for h in range(chunks):
+            bytes_of(prev.at[turn, :, span(h)], hop_recv.at[2 * turn, h])
+            damped = damp_ref[:, span(h)] * (sign_first * prev[turn, :, span(h)])
+            work[:, span(h)] = product(left_of(damped.reshape(flat)), hop_right[...]).reshape(strip)
+        hopped = product(hop_left[...], right_of(work[...].reshape(whole)))
+        forward = vec[turn].reshape(whole) - hopped
+        held[...] = forward.reshape(blocks)
+        work[...] = product(hop_left[...], right_of(forward)).reshape(blocks)
+        for h in range(chunks):
+            inner = work[:, span(h)].reshape(flat)
+            outer = product(left_of(inner), hop_right[...]).reshape(strip)
+            carr[turn, :, span(h)] = damp_ref[:, span(h)] * outer
+            push(
+                carr.at[turn, :, span(h)], foll.at[turn, :, span(h)],
+                hop_send.at[2 * turn + 1], hop_recv.at[2 * turn + 1, h], before,
+            )
+        for h in range(chunks):
+            bytes_of(foll.at[turn, :, span(h)], hop_recv.at[2 * turn + 1, h])
+            following = sign_last * foll[turn, :, span(h)]
+            rest = noise_ref[:, span(h)] - (held[:, span(h)] - following)
+            if turn == 0:
+                second[:, span(h)] = rest
+                scatter(second, slab.at[1], 4, h)
+            else:
+                res_ref[:, span(h)] = rest
 
     for turn in range(2):
         at = 4 * turn
@@ -319,7 +348,7 @@
     cosines = jnp.cos((2 * freqs + 1).astype(jnp.float32) * (math.pi / n))
     f32, bf16 = jnp.float32, jnp.bfloat16
     pair = pltpu.VMEM((2,) + blocks, f32)
-    plane = pltpu.VMEM((2, side_x, side_y), f32)
+    chunks = rows // 8
     vmem = pl.BlockSpec(memory_space=pltpu.VMEM)
     smem = pl.BlockSpec(memory_space=pltpu.SMEM)
     dma = pltpu.SemaphoreType.DMA
@@ -329,9 +358,8 @@
         out_shape=(out, out),
         in_specs=[vmem] * 4 + [smem] * 2,
         out_specs=(vmem, vmem),
-        scratch_shapes=[pair] * 7
-        + [pltpu.VMEM(blocks, f32)]
-        + [plane] * 4
+        scratch_shapes=[pair] * 11
+        + [pltpu.VMEM(blocks, f32)] * 4
         + [pltpu.VMEM((8, 128), f32), pltpu.VMEM((n, 8, 128), f32)]
         + [
             pltpu.VMEM((2 * side_x, 3 * side_x), bf16),
@@ -339,7 +367,7 @@
             pltpu.VMEM((side_x, 3 * side_x), bf16),
             pltpu.VMEM((3 * side_y, side_y), bf16),
         ]
-        + [dma((8,)), dma((8,)), dma((4,)), dma((4,)), dma(()), dma(())],
+        + [dma((8,)), dma((8, chunks)), dma((4,)), dma((4, chunks)), dma(()), dma(())],
         compiler_params=pltpu.CompilerParams(
             collective_id=0, has_side_effects=True, vmem_limit_bytes=40 * 1024 * 1024
         ),

time: 116 us -> 110 us (0.948)
  Pallas kernels: 110 us -> 104 us
    pallas_call x1, Pallas kernels: 110 us -> 104 us  [fused(): pl.pallas_call(functools.partial(fused_kernel, n), out_shape=(out, out),...]
where the time goes in v1:
time: 110 us
  Pallas kernels  104 us (95%)
  local copies, waits for them, and re-layouts  5.2 us (5%)
    pallas_call x1, Pallas kernels, fused(): pl.pallas_call(functools.partial(fused_kernel, n), out_shape=(out, out),...  104 us
    unnamed x10, local copies, waits for them, and re-layouts  5.2 us

profile of v1, /device:TPU:0, one launch (start us, length us, event | category | flops | bytes accessed | tf_op | source)
XLA Modules:
  0.0 110.1 jit_solution(11189878191330296679)
XLA Ops:
  0.7 0.1 sine_select_fusion.tab_ref
  0.8 0.0 copy-start
  0.8 0.9 copy-done
  1.8 0.0 copy-start.1
  1.8 0.9 copy-done.1
  2.7 0.0 copy-start.2
  2.7 0.9 copy-done.2
  3.7 0.0 copy-start.3
  3.7 0.9 copy-done.3
  4.6 104.0 %shard_map.59 = (f32[16,16,256]{2,1,0:T(8,128)S(1)}, f32[16,16,256]{2,1,0:T(8,128)S(1)}) custom-call(f32[16,16,256]{2,1,0:T(8,128)S(1)} %bitcast.6, s32[256,256]{1,0:T(8,128)S(1)} %bitcast.7, f32[256,256]{1,0:T(8,128)S(1)} %copy-done.2, f32[256,256]{1,0:T(8,128)S(1)} %copy-done.3, f32[16,16]{1,0:T(8,128)S(1)} %sine_select_fusion.tab_ref, ...), custom_call_target="tpu_custom_call" | custom-call | tf_op jit(solution)/shard_map/pallas_call | solution.py:356
  108.7 0.7 copy.8
  109.4 0.7 copy.9
  (3 shorter events, 0.1 us)
Async XLA Ops:
  0.8 1.0 copy-start
  1.8 0.9 copy-start.1
  2.7 0.9 copy-start.2
  3.7 0.9 copy-start.3
